TPU v7x, 512 devices: a whole 4x4x16 slice. The times are simulated.
512 devices in a mesh: seq: 64 (over x, z_lo, core), mp: 8 (over z_hi, y).
Axes of the slice: x: 4, y: 4, z: 16 (z_hi: 2, z_lo: 8; z = z_hi * 8 + z_lo), core: 2. Of those that a mesh axis runs over, the one named last changes fastest.
Arguments:
- tokens: bfloat16 [8192, 4096], P('seq', 'mp'), may hold values from -700 to 700
- norm_gain: float32 [4096], replicated, may hold values from 0.1 to 1.9
- w_qkv: bfloat16 [3, 4096, 4096], P(None, 'seq', 'mp'), may hold values from -0.09375 to 0.09375
- conv_filter: float32 [256, 128], P('mp'), may hold values from -4 to 4
- w_out: bfloat16 [4096, 4096], P('mp'), may hold values from -0.125 to 0.125
Outputs:
- mixed: bfloat16 [8192, 4096], P('seq', 'mp')
All inputs are finite; a program needn't handle non-finite values.
Results may differ from a plain program's by a relative error of at most 0.015.
Values may be sent and summed in bfloat16 or wider, within the bound.
A program may use at most 128 MiB of HBM per device.

v0:
```python
import jax
import jax.numpy as jnp
from jax import lax
from jax.sharding import PartitionSpec as P


def from_behind(value, axis, steps):
    count = lax.axis_size(axis)
    leading, last = (max(0, -steps), min(count, count - steps))
    return lax.ppermute(value, axis, [(source, source + steps) for source in range(leading, last)])


def build_toeplitz(conv_filter):
    groups, tap_count = conv_filter.shape
    reversed_f = conv_filter[:, ::-1]
    row_seq = jnp.concatenate([reversed_f, jnp.zeros((groups, tap_count + 1), jnp.float32)], axis=1)
    tiled_rows = jnp.tile(row_seq, (1, tap_count))
    return tiled_rows[:, : tap_count * 2 * tap_count].reshape(groups, tap_count, 2 * tap_count)


def local(tokens, norm_gain, w_qkv, conv_filter, w_out):
    tok_rows = tokens.shape[0]
    gathered = lax.all_gather(tokens, "mp", axis=1, tiled=True)
    gathered_f = gathered.astype(jnp.float32)
    factor = lax.rsqrt(jnp.mean(gathered_f * gathered_f, axis=1, keepdims=True) + 1e-05)
    normed = (gathered_f * factor * norm_gain).astype(jnp.bfloat16)
    channels = w_qkv.shape[2]
    full_weights = lax.all_gather(w_qkv, "seq", axis=1, tiled=True)
    projected = jnp.einsum("td,kdc->ktc", normed, full_weights, preferred_element_type=jnp.float32)
    qkv_proj = projected.astype(jnp.bfloat16)
    kv_prod = (qkv_proj[1].astype(jnp.float32) * qkv_proj[2].astype(jnp.float32)).astype(
        jnp.bfloat16
    )
    groups, tap_count = conv_filter.shape
    group_ch = channels // groups
    previous = from_behind(kv_prod[tok_rows - (tap_count - 1) :], "seq", 1)
    extended = jnp.concatenate([previous, kv_prod, jnp.zeros((1, channels), jnp.bfloat16)], axis=0)
    blocks = tok_rows // tap_count
    stacked = extended.reshape(blocks + 1, tap_count, channels)
    windows = jnp.concatenate([stacked[:-1], stacked[1:]], axis=1)
    windows_f = windows.astype(jnp.float32).reshape(blocks, 2 * tap_count, groups, group_ch)
    toeplitz = build_toeplitz(conv_filter)
    convolved = jnp.einsum("gij,bjgc->bigc", toeplitz, windows_f, precision=lax.Precision.HIGHEST)
    convolved = convolved.reshape(tok_rows, channels)
    gated_out = (qkv_proj[0].astype(jnp.float32) * convolved).astype(jnp.bfloat16)
    mixed_t = lax.psum_scatter(
        jnp.einsum("cd,tc->dt", w_out, gated_out, preferred_element_type=jnp.float32).astype(
            jnp.bfloat16
        ),
        "mp",
        scatter_dimension=0,
        tiled=True,
    ).astype(jnp.float32)
    return mixed_t.T.astype(jnp.bfloat16)


def solution(mesh):
    placed = (P("seq", "mp"), P(), P(None, "seq", "mp"), P("mp", None), P("mp", None))
    return jax.shard_map(
        local, mesh=mesh, in_specs=placed, out_specs=P("seq", "mp"), check_vma=False
    )
```

profile of v0, /device:TPU:1, one launch (start us, length us, event | category | flops | bytes accessed | tf_op | source)
XLA Modules:
  0.0 379.5 jit_solution(15595742339285763453)
XLA Ops:
  6.5 0.0 all-gather.3.cloned.1.call-start
  6.5 0.7 all-gather.3.cloned.1.call-update
  7.3 0.0 all-gather.5.cloned.1.call-start
  7.3 0.7 all-gather.5.cloned.1.call-update
  8.0 0.0 reduce-scatter.2.cloned.1.call-start
  8.1 0.8 rev.3
  8.8 3.0 tile.4
  11.9 6.7 %tile.10 = f32[32,32896]{1,0:T(8,128)} reshape(f32[32,128,257]{2,1,0:T(8,128)} %tile.4) | data formatting | bytes 8421376 | tf_op jit(solution)/shard_map/tile | solution.py:17
  18.5 0.0 slice-start
  18.5 2.2 slice-done
  20.7 0.0 copy-start
  20.7 3.2 copy.12
  23.9 79.2 %all-gather.3.cloned.1.call-done = bf16[128,4096]{1,0:T(8,128)(2,1)} async-done(((bf16[128,512]{1,0:T(8,128)(2,1)}), bf16[128,4096]{1,0:T(8,128)(2,1)}) %all-gather.3.cloned.1.call-update) | async-done | bytes 1048592 | tf_op jit(solution)/shard_map/all_gather | solution.py:23
  103.1 1.5 fusion.1
  104.7 127.5 %all-gather.5.cloned.1.call-done = bf16[3,4096,512]{2,1,0:T(8,128)(2,1)} async-done(((bf16[3,64,512]{2,1,0:T(8,128)(2,1)}), bf16[3,4096,512]{2,1,0:T(8,128)(2,1)}) %all-gather.5.cloned.1.call-update) | async-done | bytes 12582928 | tf_op jit(solution)/shard_map/all_gather | solution.py:28
  232.1 0.0 copy-done
  232.1 6.8 %fusion.4 = bf16[3,128,512]{2,1,0:T(8,128)(2,1)S(1)} fusion(bf16[3,4096,512]{2,1,0:T(8,128)(2,1)} %all-gather.5.cloned.1.call-done, bf16[128,4096]{1,0:T(8,128)(2,1)} %all-gather.3.cloned.1.call-done, f32[4096]{0:T(1024)S(1)} %copy-done, f32[128]{0:T(128)S(1)} %add_rsqrt_fusion), kind=kOutput, calls=%fused_computation.8 | convolution fusion | flops 1612906496 | bytes 14041600 | tf_op jit(solution)/shard_map/td,kdc->ktc/dot_general | solution.py:29
  239.0 3.1 collective-permute-start
  242.1 1.9 collective-permute-done
  244.1 0.1 copy.9
  244.2 0.1 copy.10
  244.3 4.2 %fusion.9 = f32[32,16,128]{2,1,0:T(8,128)S(1)} fusion(f32[32,128,256]{2,1,0:T(8,128)} %bitcast.34, bf16[1,128,32,16]{1,3,2,0:T(8,128)(2,1)S(1)} %bitcast.37, bf16[1,128,32,16]{1,3,2,0:T(8,128)(2,1)S(1)} %bitcast.36), kind=kOutput, calls=%fused_computation.13 | convolution fusion | flops 201850880 | bytes 4718592 | tf_op jit(solution)/shard_map/gij,bjgc->bigc/dot_general | solution.py:43
  248.5 0.1 copy.11
  248.6 3.9 %fusion = bf16[4096,128]{0,1:T(8,128)(2,1)} fusion(bf16[512,4096]{1,0:T(8,128)(2,1)} %param.9, f32[128,512]{1,0:T(8,128)S(1)} %copy.11, bf16[3,128,512]{2,1,0:T(8,128)(2,1)S(1)} %fusion.4), kind=kOutput, calls=%fused_computation.1 | convolution fusion | flops 537591808 | bytes 5636096 | tf_op jit(solution)/shard_map/cd,tc->dt/dot_general | solution.py:47
  252.5 0.0 reduce-scatter.2.cloned.1.call-update
  252.5 120.4 %reduce-scatter.2.cloned.1.call-done = bf16[512,128]{0,1:T(8,128)(2,1)} async-done(((bf16[4096,128]{0,1:T(8,128)(2,1)}), bf16[512,128]{0,1:T(8,128)(2,1)}) %reduce-scatter.2.cloned.1.call-update) | async-done | bytes 131088 | tf_op jit(solution)/shard_map/reduce_scatter | solution.py:46
  (6 shorter events, 0.2 us)
Async XLA Ops:
  6.5 96.6 %all-gather.3.cloned.1.call-start = ((), (), s32[]{:S(2)}) async-start(), calls=%async_computation.1 | async-start | bytes 1179648 | tf_op jit(solution)/shard_map/all_gather | solution.py:23
  7.3 224.9 %all-gather.5.cloned.1.call-start = ((), (), s32[]{:S(2)}) async-start(), calls=%async_computation.2 | async-start | bytes 12779520 | tf_op jit(solution)/shard_map/all_gather | solution.py:28
  8.0 365.0 %reduce-scatter.2.cloned.1.call-start = ((), (), s32[]{:S(2)}) async-start(), calls=%async_computation.3 | async-start | bytes 1179648 | tf_op jit(solution)/shard_map/reduce_scatter | solution.py:46
  18.5 2.2 slice-start
  20.7 211.4 %copy-start = (f32[4096]{0:T(1024)S(1)}, f32[4096]{0:T(1024)}, u32[]{:S(2)}) copy-start(f32[4096]{0:T(1024)} %param.6) | copy-start | bytes 49156
  239.0 5.0 %collective-permute-start = (bf16[127,512]{1,0:T(8,128)(2,1)S(1)}, bf16[127,512]{1,0:T(8,128)(2,1)S(1)}, u32[]{:S(2)}, u32[]{:S(2)}) collective-permute-start(bf16[127,512]{1,0:T(8,128)(2,1)S(1)} %slice_bitcast_fusion), channel_id=1, source_target_pairs={{0,8},{8,16},{16,24},{24,32},{32,40},{40,48},{48,56},{56,64},{64,7... | collective-permute-start | bytes 390152 | tf_op jit(solution)/shard_map/ppermute | solution.py:10
Sparse Core Ops, SparseCore 0:
  10.4 92.6 all-gather.2
  105.3 126.7 all-gather.4
  252.6 120.2 reduce-scatter.1
where the time goes:
time: 380 us; the launch traced here: 379 us
  waiting for transfers between devices  330 us (87%)
  local copies, waits for them, and re-layouts  16.3 us (4%)
  matrix products  14.8 us (4%)
  between operations  13.2 us (3%)
    all_gather x1, waiting for transfers between devices, local(): full_weights = lax.all_gather(w_qkv, 'seq', axis=1, tiled=True)  127 us
    reduce_scatter x1, waiting for transfers between devices, local(): lax.psum_scatter(jnp.einsum('cd,tc->dt', w_out, gated_out, preferred_elem...  120 us
    all_gather x1, waiting for transfers between devices, local(): gathered = lax.all_gather(tokens, 'mp', axis=1, tiled=True)  79.2 us
    another operation x2, local copies, waits for them, and re-layouts, build_toeplitz(): tiled_rows = jnp.tile(row_seq, (1, tap_count))  9.67 us
  transfers between devices with their start and end apart: 4, of which 4 were waited for; matrix products, arithmetic and copies ran while one was open for 4% of the time, Pallas kernels for 0%

commit v1 on v0

v1 whole, which is shorter than its diff:
```python
import functools

import jax
import jax.numpy as jnp
from jax import lax
from jax.experimental import pallas as pl
from jax.experimental.pallas import tpu as pltpu
from jax.sharding import PartitionSpec as P

NX, NZ, NY = 4, 8, 4
TAPS = 128
LAG_X, LAG_H = 3, 4
F32, BF16 = jnp.float32, jnp.bfloat16


def dot(a, b):
    return jnp.dot(a, b, preferred_element_type=F32)


def kernel(
    tok_in, gain, w_in, filt, wout_in, out,
    wbuf, tok, normed, acc, kvb, halo, frev, tcur, tprev, wout, part, peers, zsum, zpeer,
    loc, z_s, z_r, x_s, x_r, h_s, h_r, d_s, d_r, tz_s, tz_r, ty_s, ty_r, hl_s, hl_r, rs_s, rs_r, rz_s, rz_r,
):
    seq, mp = lax.axis_index("seq"), lax.axis_index("mp")
    core, p, x = seq % 2, (seq // 2) % NZ, seq // (2 * NZ)
    zhi, y = mp // NY, mp % NY
    rows = tok_in.shape[0]
    depth = w_in.shape[1]
    width = w_in.shape[2]
    column = 2 * NZ * depth
    sibling = (seq + 1 - 2 * core, mp)
    across = (seq, (mp + NY) % (2 * NY))
    n_seq = 2 * NZ * NX

    def along_x(d):
        return ((seq + (2 * NZ if d == 0 else n_seq - 2 * NZ)) % n_seq, mp)

    def along_z(d):
        return (seq + (2 if d == 0 else -2), mp)

    def along_y(o):
        return (seq, zhi * NY + (y + o) % NY)

    def remote(src, dst, s, r, dev):
        return pltpu.make_async_remote_copy(
            src_ref=src, dst_ref=dst, send_sem=s, recv_sem=r,
            device_id=dev, device_id_type=pl.DeviceIdType.MESH,
        )

    own_w = pl.ds(pl.multiple_of(seq * depth, depth), depth)
    load_tok = pltpu.make_async_copy(tok_in, tok.at[mp], loc.at[0])
    load_w = pltpu.make_async_copy(w_in, wbuf.at[:, own_w, :], loc.at[1])
    load_wout = pltpu.make_async_copy(wout_in, wout, loc.at[2])
    load_tok.start()
    load_w.start()
    load_wout.start()

    barrier = pltpu.get_barrier_semaphore()

    def greet(dev):
        pl.semaphore_signal(barrier, inc=1, device_id=dev, device_id_type=pl.DeviceIdType.MESH)

    for dev in (along_x(0), along_x(1), sibling, across, along_y(1), along_y(2), along_y(3)):
        greet(dev)
    has_up, has_down = p < NZ - 1, p > 0
    has_far = jnp.where(core == 0, seq > 0, seq < n_seq - 1)
    far = jnp.where(core == 0, seq - 1, seq + 1)

    @pl.when(has_up)
    def _():
        greet(along_z(0))

    @pl.when(has_down)
    def _():
        greet(along_z(1))

    @pl.when(has_far)
    def _():
        greet((far, mp))

    load_tok.wait()
    load_w.wait()
    pl.semaphore_wait(
        barrier, 7 + has_up.astype(jnp.int32) + has_down.astype(jnp.int32) + has_far.astype(jnp.int32)
    )

    tok_z = remote(tok.at[mp], tok.at[mp], tz_s.at[0], tz_r.at[0], across)
    tok_z.start()

    def tok_y(half, o):
        m = mp if half == 0 else (mp + NY) % (2 * NY)
        return remote(tok.at[m], tok.at[m], ty_s.at[half, o - 1], ty_r.at[half, o - 1], along_y(o))

    def tok_y_arrival(half, o):
        m = (zhi if half == 0 else 1 - zhi) * NY + (y + NY - o) % NY
        return remote(tok.at[m], tok.at[m], ty_s.at[half, o - 1], ty_r.at[half, o - 1], along_y(o))

    for o in (2, 1, 3):
        tok_y(0, o).start()

    def block(xx, j, c):
        return wbuf.at[:, pl.ds(pl.multiple_of(((xx * NZ + j) * 2 + c) * depth, depth), depth), :]

    def half_block(xx, j, c, h):
        at = ((xx * NZ + j) * 2 + c) * depth + h * (depth // 2)
        return wbuf.at[:, pl.ds(pl.multiple_of(at, depth // 2), depth // 2), :]

    def z_copy(d, j):
        return remote(block(x, j, core), block(x, j, core), z_s.at[d, j], z_r.at[j], along_z(d))

    def x_copy(d, xx, j):
        return remote(block(xx, j, core), block(xx, j, core), x_s.at[d, j], x_r.at[d, j], along_x(d))

    def h_copy(d, xx, j):
        ref = half_block(xx, j, core, d)
        return remote(ref, ref, h_s.at[d, j], h_r.at[d, j], along_x(d))

    def d_copy(k, j, c):
        ref = block((x + k) % NX, j, c)
        return remote(ref, ref, d_s.at[k, j], d_r.at[k, j], sibling)

    fewer = jnp.minimum(p, NZ - 1 - p)

    def nth(n):
        paired = jnp.where(n % 2 == 1, p - (n + 1) // 2, p + (n + 1) // 2)
        rest = jnp.where(2 * p < NZ, p + n - fewer, p - n + fewer)
        return jnp.where(n <= 2 * fewer, paired, rest)

    def stage_z(n):
        j = nth(n)

        @pl.when(n > 0)
        def _():
            z_copy(0, j).wait_recv()

        @pl.when(has_up & (j <= p))
        def _():
            z_copy(0, j).start()

        @pl.when(has_down & (j >= p))
        def _():
            z_copy(1, j).start()

        x_copy(0, x, j).start()
        x_copy(1, x, j).start()
        d_copy(0, j, core).start()

    def stage_x(n):
        j = nth(n)
        left, right = (x + NX - 1) % NX, (x + 1) % NX
        x_copy(0, left, j).wait_recv()
        h_copy(0, left, j).start()
        d_copy(3, j, core).start()
        x_copy(1, right, j).wait_recv()
        h_copy(1, right, j).start()
        d_copy(1, j, core).start()

    def stage_h(n):
        j = nth(n)
        opposite = (x + 2) % NX
        h_copy(0, opposite, j).wait_recv()
        h_copy(1, opposite, j).wait_recv()
        d_copy(2, j, core).start()

    def steps(first, last):
        def step(n, carry):
            @pl.when(n < NZ)
            def _():
                stage_z(n)

            @pl.when((n >= LAG_X) & (n < NZ + LAG_X))
            def _():
                stage_x(n - LAG_X)

            @pl.when(n >= LAG_H)
            def _():
                stage_h(n - LAG_H)

            return carry

        lax.fori_loop(first, last, step, 0)

    def from_sibling(k):
        def one(j, carry):
            d_copy(k, j, 1 - core).wait_recv()
            return carry

        lax.fori_loop(0, NZ, one, 0)

    steps(0, 1)

    lane = lax.broadcasted_iota(jnp.int32, (TAPS, TAPS), 1)
    row = lax.broadcasted_iota(jnp.int32, (TAPS, TAPS), 0)
    flip = jnp.where(lane + row == TAPS - 1, 1.0, 0.0).astype(BF16)
    frev[...] = dot(filt[...].astype(BF16), flip)

    def build(g, carry):
        spread = jnp.broadcast_to(frev[pl.ds(g, 1), :], (TAPS, TAPS))
        turned = pltpu.roll(spread, 1, 1, stride=1, stride_axis=0)
        tcur[g] = jnp.where(lane <= row, turned, 0.0).astype(BF16)
        tprev[g] = jnp.where(lane > row, turned, 0.0).astype(BF16)
        return carry

    lax.fori_loop(0, filt.shape[0], build, 0)

    steps(1, 3)
    tok_z.wait_recv()
    for o in (2, 1, 3):
        tok_y(1, o).start()
    steps(3, 6)

    for half in range(2):
        for o in (1, 2, 3):
            tok_y_arrival(half, o).wait_recv()
    squares = jnp.zeros((rows, 128), F32)
    for m in range(2 * NY):
        for c in range(width // 128):
            v = tok[m, :, c * 128 : (c + 1) * 128].astype(F32)
            squares = squares + v * v
    factor = lax.rsqrt(jnp.sum(squares, axis=1, keepdims=True) / (2 * NY * width) + 1e-05)
    per = column // width
    for m in range(2 * NY):
        v = tok[m].astype(F32) * factor * gain[:, m * width : (m + 1) * width]
        normed[m // per, :, (m % per) * width : (m % per + 1) * width] = v.astype(BF16)

    def weights(i, xx):
        return wbuf[i, pl.ds(pl.multiple_of(xx * column, column), column), :]

    def multiply(k):
        xx = (x + k) % NX
        for i in range(2):
            product = dot(normed[xx], weights(1 + i, xx))
            if k == 0:
                acc[i] = product
            else:
                acc[i] += product

    steps(6, NZ)
    from_sibling(0)
    multiply(0)
    steps(NZ, NZ + LAG_X)
    from_sibling(3)
    multiply(3)
    from_sibling(1)
    multiply(1)
    steps(NZ + LAG_X, NZ + LAG_H)
    from_sibling(2)
    multiply(2)

    key, value = acc[0].astype(BF16).astype(F32), acc[1].astype(BF16).astype(F32)
    kvb[...] = (key * value).astype(BF16)
    hand_on = remote(kvb, halo, hl_s.at[0], hl_r.at[0], ((seq + 1) % n_seq, mp))

    @pl.when(seq < n_seq - 1)
    def _():
        hand_on.start()

    @pl.when(seq == 0)
    def _():
        halo[...] = jnp.zeros_like(halo)

    q = dot(normed[0], weights(0, 0))
    for xx in range(1, NX):
        q = q + dot(normed[xx], weights(0, xx))
    acc[0] = q.astype(BF16).astype(F32)

    groups = filt.shape[0]
    of_lane = lane // (width // groups)
    per_tile = 128 // (width // groups)

    def convolve(mats, source, t):
        lhs = mats[t * per_tile : (t + 1) * per_tile].reshape(per_tile * TAPS, TAPS)
        wide = dot(lhs, source[:, t * 128 : (t + 1) * 128])
        total = jnp.zeros((TAPS, 128), F32)
        for g in range(per_tile):
            total = jnp.where(of_lane == g, wide[g * TAPS : (g + 1) * TAPS], total)
        return total

    for t in range(width // 128):
        acc[1, :, t * 128 : (t + 1) * 128] = convolve(tcur, kvb, t)

    @pl.when(seq > 0)
    def _():
        hand_on.wait_recv()

    for t in range(width // 128):
        at = slice(t * 128, (t + 1) * 128)
        convolved = acc[1, :, at] + convolve(tprev, halo, t)
        normed[0, :, at] = (acc[0, :, at] * convolved).astype(BF16)

    load_wout.wait()
    gated = normed[0, :, :width]

    def share(m):
        return dot(gated, wout[:, pl.ds(pl.multiple_of(m * width, width), width)])

    def exchange(o, zsel):
        m = (zhi if zsel == 1 else 1 - zhi) * NY + (y + o) % NY
        return remote(part.at[o - 1, zsel], peers.at[o - 1, zsel], rs_s.at[o - 1, zsel], rs_r.at[o - 1, zsel], along_y(o)), m

    for zsel in range(2):
        for o in (2, 1, 3):
            copy, m = exchange(o, zsel)
            part[o - 1, zsel] = share(m).astype(BF16)
            copy.start()
    acc[0] = share((1 - zhi) * NY + y).astype(BF16).astype(F32)
    for o in (1, 3, 2):
        exchange(o, 0)[0].wait_recv()
    zsum[...] = (acc[0] + peers[0, 0].astype(F32) + peers[1, 0].astype(F32) + peers[2, 0].astype(F32)).astype(BF16)
    cross = remote(zsum, zpeer, rz_s.at[0], rz_r.at[0], across)
    cross.start()
    acc[1] = share(mp).astype(BF16).astype(F32)
    for o in (1, 3, 2):
        exchange(o, 1)[0].wait_recv()
    acc[1] = acc[1] + peers[0, 1].astype(F32) + peers[1, 1].astype(F32) + peers[2, 1].astype(F32)

    def sent(j, carry):
        @pl.when(has_up & (j <= p))
        def _():
            z_copy(0, j).wait_send()

        @pl.when(has_down & (j >= p))
        def _():
            z_copy(1, j).wait_send()

        for d in range(2):
            x_copy(d, x, j).wait_send()
            h_copy(d, x, j).wait_send()
        for k in range(NX):
            d_copy(k, j, core).wait_send()
        return carry

    lax.fori_loop(0, NZ, sent, 0)
    tok_z.wait_send()
    for half in range(2):
        for o in (1, 2, 3):
            tok_y(half, o).wait_send()
    for zsel in range(2):
        for o in (1, 2, 3):
            exchange(o, zsel)[0].wait_send()

    @pl.when(seq < n_seq - 1)
    def _():
        hand_on.wait_send()

    cross.wait()
    out[...] = (acc[1] + zpeer[...].astype(F32)).astype(BF16)


def local(tokens, norm_gain, w_qkv, conv_filter, w_out):
    rows, width = tokens.shape
    features = norm_gain.shape[0]
    depth = w_qkv.shape[1]
    groups = conv_filter.shape[0]
    dma = pltpu.SemaphoreType.DMA
    column = 2 * NZ * depth
    scratch = [
        pltpu.VMEM((3, features, width), BF16),
        pltpu.VMEM((2 * NY, rows, width), BF16),
        pltpu.VMEM((NX, rows, column), BF16),
        pltpu.VMEM((2, rows, width), F32),
        pltpu.VMEM((rows, width), BF16),
        pltpu.VMEM((rows, width), BF16),
        pltpu.VMEM((groups, TAPS), F32),
        pltpu.VMEM((groups, TAPS, TAPS), BF16),
        pltpu.VMEM((groups, TAPS, TAPS), BF16),
        pltpu.VMEM(w_out.shape, BF16),
        pltpu.VMEM((NY - 1, 2, rows, width), BF16),
        pltpu.VMEM((NY - 1, 2, rows, width), BF16),
        pltpu.VMEM((rows, width), BF16),
        pltpu.VMEM((rows, width), BF16),
    ]
    sems = [(3,), (2, NZ), (NZ,), (2, NZ), (2, NZ), (2, NZ), (2, NZ), (NX, NZ), (NX, NZ)]
    sems += [(1,), (1,), (2, NY - 1), (2, NY - 1), (1,), (1,), (NY - 1, 2), (NY - 1, 2), (1,), (1,)]
    hbm, vmem = pl.BlockSpec(memory_space=pl.ANY), pl.BlockSpec(memory_space=pltpu.VMEM)
    return pl.pallas_call(
        kernel,
        out_shape=jax.ShapeDtypeStruct((rows, width), BF16),
        in_specs=[hbm, vmem, hbm, vmem, hbm],
        out_specs=vmem,
        scratch_shapes=scratch + [dma(s) for s in sems],
        compiler_params=pltpu.CompilerParams(
            collective_id=0, has_side_effects=True, vmem_limit_bytes=50 * 1024 * 1024
        ),
        cost_estimate=pl.CostEstimate(flops=2300000000, bytes_accessed=20000000, transcendentals=0),
    )(tokens, norm_gain.reshape(1, features), w_qkv, conv_filter, w_out)


def solution(mesh):
    placed = (P("seq", "mp"), P(), P(None, "seq", "mp"), P("mp", None), P("mp", None))
    return jax.shard_map(
        local, mesh=mesh, in_specs=placed, out_specs=P("seq", "mp"), check_vma=False
    )
```

time: 380 us -> 123 us (0.32)
  waiting for transfers between devices: 330 us -> 0 us
  Pallas kernels: 0 us -> 119 us
  matrix products: 14.8 us -> 0 us
  between operations: 13.2 us -> 0.01 us
  local copies, waits for them, and re-layouts: 16.3 us -> 3.92 us
    all_gather x2 -> x0, waiting for transfers between devices: 207 us -> none  [the longest x1 127 us: local(): full_weights = lax.all_gather(w_qkv, 'seq', axis=1, tiled=True)]
    reduce_scatter x1 -> x0, waiting for transfers between devices: 120 us -> none  [local(): lax.psum_scatter(jnp.einsum('cd,tc->dt', w_out, gated_out, preferred_elem...]
    pallas_call x0 -> x1, Pallas kernels: none -> 119 us  [local(): pl.pallas_call(kernel, out_shape=jax.ShapeDtypeStruct((rows, width), BF16...]
    dot_general x3 -> x0, matrix products: 14.8 us -> none  [the longest x1 6.75 us: local(): jnp.einsum('td,kdc->ktc', normed, full_weights, preferred_element_type=jn...]
    another operation x2 -> x0, local copies, waits for them, and re-layouts: 9.67 us -> none  [build_toeplitz(): tiled_rows = jnp.tile(row_seq, (1, tap_count))]
  transfers between devices with their start and end apart: 4 -> 0, of which waited for: 4 -> 0; matrix products, arithmetic and copies ran while one was open for 4% -> 0% of each run, Pallas kernels for 0% -> 0%
where the time goes in v1:
time: 123 us
  Pallas kernels  119 us (97%)
  local copies, waits for them, and re-layouts  3.92 us (3%)
    pallas_call x1, Pallas kernels, local(): pl.pallas_call(kernel, out_shape=jax.ShapeDtypeStruct((rows, width), BF16...  119 us
    unnamed x9, local copies, waits for them, and re-layouts  3.92 us

profile of v1, /device:TPU:1, one launch (start us, length us, event | category | flops | bytes accessed | tf_op | source)
XLA Modules:
  0.0 123.1 jit_solution(7239296837965893187)
XLA Ops:
  0.0 0.0 copy-start
  0.0 0.9 copy-done
  0.9 0.0 copy-start.1
  0.9 0.9 copy-done.1
  1.8 0.0 copy-start.2
  1.8 0.7 copy-done.2
  2.6 0.0 copy-start.3
  2.6 0.7 copy-done.3
  3.3 119.2 %shard_map.55 = bf16[128,512]{1,0:T(8,128)(2,1)S(1)} custom-call(bf16[128,512]{1,0:T(8,128)(2,1)S(1)} %copy-done.1, f32[1,4096]{1,0:T(1,128)S(1)} %bitcast.1, bf16[3,64,512]{2,1,0:T(8,128)(2,1)S(1)} %copy-done, f32[32,128]{1,0:T(8,128)S(1)} %copy-done.3, bf16[512,4096]{1,0:T(8,128)(2,1)} %wout_in.1), custom_call_target="tpu_custom_call" | custom-call | flops 2300000000 | bytes 20000000 | tf_op jit(solution)/shard_map/pallas_call | solution.py:377
  122.5 0.7 copy.7
Async XLA Ops:
  0.0 0.9 copy-start
  0.9 0.9 copy-start.1
  1.8 0.7 copy-start.2
  2.6 0.7 copy-start.3

commit v2 on v1

v2 whole, which is shorter than its diff:
```python
import functools

import jax
import jax.numpy as jnp
from jax import lax
from jax.experimental import pallas as pl
from jax.experimental.pallas import tpu as pltpu
from jax.sharding import PartitionSpec as P

NX, NZ, NY = 4, 8, 4
TAPS = 128
SPLIT = 2
F32, BF16 = jnp.float32, jnp.bfloat16


def dot(a, b):
    return jnp.dot(a, b, preferred_element_type=F32)


def kernel(
    tok_in, gain_in, w_in, filt_in, wout_in, out,
    wbuf, tok, normed, acc, kvb, halo, gain, filt, frev, tcur, tprev, wout, part, peers, zsum, zpeer,
    loc, z_s, z_r, x_s, x_r, d_s, d_r, own_r, tz_s, tz_r, ty_s, ty_r, hl_s, hl_r, rs_s, rs_r, rz_s, rz_r,
):
    seq, mp = lax.axis_index("seq"), lax.axis_index("mp")
    core, p, x = seq % 2, (seq // 2) % NZ, seq // (2 * NZ)
    zhi, y = mp // NY, mp % NY
    rows = tok_in.shape[0]
    depth = w_in.shape[1]
    width = w_in.shape[2]
    chunk = 2 * depth
    column = NZ * chunk
    cut = width // SPLIT
    sibling = (seq + 1 - 2 * core, mp)
    across = (seq, (mp + NY) % (2 * NY))
    n_seq = 2 * NZ * NX

    def along_x(k):
        return ((seq + 2 * NZ * k) % n_seq, mp)

    def along_z(d):
        return (seq + (2 if d == 0 else -2), mp)

    def along_y(o):
        return (seq, zhi * NY + (y + o) % NY)

    def remote(src, dst, s, r, dev):
        return pltpu.make_async_remote_copy(
            src_ref=src, dst_ref=dst, send_sem=s, recv_sem=r,
            device_id=dev, device_id_type=pl.DeviceIdType.MESH,
        )

    own_w = pl.ds(pl.multiple_of(seq * depth, depth), depth)
    loads = [
        pltpu.make_async_copy(filt_in, filt, loc.at[0]),
        pltpu.make_async_copy(tok_in, tok.at[mp], loc.at[1]),
        pltpu.make_async_copy(w_in, wbuf.at[:, own_w, :], loc.at[2]),
        pltpu.make_async_copy(gain_in, gain, loc.at[3]),
        pltpu.make_async_copy(wout_in, wout, loc.at[4]),
    ]
    for load in loads:
        load.start()

    barrier = pltpu.get_barrier_semaphore()

    def greet(dev):
        pl.semaphore_signal(barrier, inc=1, device_id=dev, device_id_type=pl.DeviceIdType.MESH)

    for dev in [sibling, across] + [along_x(k) for k in (1, 2, 3)] + [along_y(o) for o in (1, 2, 3)]:
        greet(dev)
    has_up, has_down = p < NZ - 1, p > 0
    has_far = jnp.where(core == 0, seq > 0, seq < n_seq - 1)
    far = jnp.where(core == 0, seq - 1, seq + 1)

    @pl.when(has_up)
    def _():
        greet(along_z(0))

    @pl.when(has_down)
    def _():
        greet(along_z(1))

    @pl.when(has_far)
    def _():
        greet((far, mp))

    lane = lax.broadcasted_iota(jnp.int32, (TAPS, TAPS), 1)
    row = lax.broadcasted_iota(jnp.int32, (TAPS, TAPS), 0)
    flip = jnp.where(lane + row == TAPS - 1, 1.0, 0.0).astype(BF16)
    loads[0].wait()
    frev[...] = dot(filt[...].astype(BF16), flip)

    def build(g, carry):
        spread = jnp.broadcast_to(frev[pl.ds(g, 1), :], (TAPS, TAPS))
        turned = pltpu.roll(spread, 1, 1, stride=1, stride_axis=0)
        tcur[g] = jnp.where(lane <= row, turned, 0.0).astype(BF16)
        tprev[g] = jnp.where(lane > row, turned, 0.0).astype(BF16)
        return carry

    lax.fori_loop(0, filt.shape[0], build, 0)
    for load in loads[1:4]:
        load.wait()
    pl.semaphore_wait(
        barrier, 8 + has_up.astype(jnp.int32) + has_down.astype(jnp.int32) + has_far.astype(jnp.int32)
    )

    tok_z = remote(tok.at[mp], tok.at[mp], tz_s.at[0], tz_r.at[0], across)
    tok_z.start()

    def tok_y(half, o):
        m = mp if half == 0 else (mp + NY) % (2 * NY)
        return remote(tok.at[m], tok.at[m], ty_s.at[half, o - 1], ty_r.at[half, o - 1], along_y(o))

    def tok_y_arrival(half, o):
        m = (zhi if half == 0 else 1 - zhi) * NY + (y + NY - o) % NY
        return remote(tok.at[m], tok.at[m], ty_s.at[half, o - 1], ty_r.at[half, o - 1], along_y(o))

    for o in (2, 1, 3):
        tok_y(0, o).start()

    def rows_of(piece, start, count):
        which = pl.ds(1, 2) if piece == 0 else pl.ds(0, 1)
        return wbuf.at[which, pl.ds(pl.multiple_of(start, depth), count), :]

    def block(piece, xx, j, c):
        return rows_of(piece, ((xx * NZ + j) * 2 + c) * depth, depth)

    def z_copy(piece, d, j):
        ref = block(piece, x, j, core)
        return remote(ref, ref, z_s.at[piece, d, j], z_r.at[piece, j], along_z(d))

    def x_copy(piece, k, xx, j):
        ref = block(piece, xx, j, core)
        return remote(ref, ref, x_s.at[piece, k - 1], x_r.at[piece, k - 1, j], along_x(k))

    def d_copy(piece, k, j, c):
        ref = block(piece, (x + k) % NX, j, c)
        arrived = own_r.at[piece] if k == 0 else d_r.at[piece, k - 1, j]
        return remote(ref, ref, d_s.at[piece], arrived, sibling)

    fewer = jnp.minimum(p, NZ - 1 - p)

    def nth(n):
        paired = jnp.where(n % 2 == 1, p - (n + 1) // 2, p + (n + 1) // 2)
        rest = jnp.where(2 * p < NZ, p + n - fewer, p - n + fewer)
        return jnp.where(n <= 2 * fewer, paired, rest)

    def stage_z(piece, n):
        j = nth(n)

        @pl.when(n > 0)
        def _():
            z_copy(piece, 0, j).wait_recv()

        @pl.when(has_up & (j <= p))
        def _():
            z_copy(piece, 0, j).start()

        @pl.when(has_down & (j >= p))
        def _():
            z_copy(piece, 1, j).start()

        for k in (2, 1, 3):
            x_copy(piece, k, x, j).start()
        d_copy(piece, 0, j, core).start()

    def stage_x(piece, n):
        j = nth(n)
        for k in (1, 3, 2):
            x_copy(piece, k, (x + NX - k) % NX, j).wait_recv()
            d_copy(piece, NX - k, j, core).start()

    def loop(first, last, *stages):
        def step(n, carry):
            for stage in stages:
                stage(n)
            return carry

        lax.fori_loop(first, last, step, 0)

    loop(0, 4, functools.partial(stage_z, 0))
    tok_z.wait_recv()
    for o in (2, 1, 3):
        tok_y(1, o).start()
    loop(4, NZ, functools.partial(stage_z, 0))

    for half in range(2):
        for o in (1, 2, 3):
            tok_y_arrival(half, o).wait_recv()
    squares = jnp.zeros((rows, 128), F32)
    for m in range(2 * NY):
        for c in range(width // 128):
            v = tok[m, :, c * 128 : (c + 1) * 128].astype(F32)
            squares = squares + v * v
    factor = lax.rsqrt(jnp.sum(squares, axis=1, keepdims=True) / (2 * NY * width) + 1e-05)
    per = column // width
    for m in range(2 * NY):
        v = tok[m].astype(F32) * factor * gain[:, m * width : (m + 1) * width]
        normed[m // per, :, (m % per) * width : (m % per + 1) * width] = v.astype(BF16)

    def multiply_own(piece):
        whole = rows_of(piece, x * column, NZ * depth)
        remote(whole, whole, d_s.at[piece], own_r.at[piece], sibling).wait_recv()
        at = pl.ds(pl.multiple_of(x * column, column), column)
        for i in (1, 2) if piece == 0 else (0,):
            acc[i] = dot(normed[x], wbuf[i, at, :])

    def multiply(piece, n):
        j = nth(n)
        lhs, at = [], []
        for k in (1, 2, 3):
            d_copy(piece, k, j, 1 - core).wait_recv()
            xx = (x + k) % NX
            lhs.append(normed[xx, :, pl.ds(pl.multiple_of(j * chunk, chunk), chunk)])
            at.append(pl.ds(pl.multiple_of((xx * NZ + j) * chunk, chunk), chunk))
        lhs = jnp.concatenate(lhs, axis=1)
        for i in (1, 2) if piece == 0 else (0,):
            acc[i] += dot(lhs, jnp.concatenate([wbuf[i, a, :] for a in at], axis=0))

    def late(piece):
        def stage(n):
            @pl.when(n > 0)
            def _():
                multiply(piece, n - 1)

        return stage

    multiply_own(0)
    loop(0, NZ, functools.partial(stage_x, 0), functools.partial(stage_z, 1), late(0))
    multiply(0, NZ - 1)

    key, value = acc[1].astype(BF16).astype(F32), acc[2].astype(BF16).astype(F32)
    kvb[...] = (key * value).astype(BF16)
    hand_on = remote(kvb, halo, hl_s.at[0], hl_r.at[0], ((seq + 1) % n_seq, mp))

    @pl.when(seq < n_seq - 1)
    def _():
        hand_on.start()

    @pl.when(seq == 0)
    def _():
        halo[...] = jnp.zeros_like(halo)

    groups = filt.shape[0]
    of_lane = lane // (width // groups)
    per_tile = 128 // (width // groups)

    def convolve(mats, source, t):
        lhs = mats[t * per_tile : (t + 1) * per_tile].reshape(per_tile * TAPS, TAPS)
        wide = dot(lhs, source[:, t * 128 : (t + 1) * 128])
        total = jnp.zeros((TAPS, 128), F32)
        for g in range(per_tile):
            total = jnp.where(of_lane == g, wide[g * TAPS : (g + 1) * TAPS], total)
        return total

    for t in range(width // 128):
        acc[1, :, t * 128 : (t + 1) * 128] = convolve(tcur, kvb, t)
    multiply_own(1)
    loop(0, 4, functools.partial(stage_x, 1), late(1))

    @pl.when(seq > 0)
    def _():
        hand_on.wait_recv()

    for t in range(width // 128):
        acc[1, :, t * 128 : (t + 1) * 128] += convolve(tprev, halo, t)
    loads[4].wait()
    loop(4, NZ, functools.partial(stage_x, 1), late(1))
    multiply(1, NZ - 1)
    gated = (acc[0].astype(BF16).astype(F32) * acc[1]).astype(BF16)
    normed[0, :, :width] = gated

    def share(m, c):
        return dot(normed[0, :, :width], wout[:, pl.ds(pl.multiple_of(m * width + c * cut, cut), cut)])

    def exchange(o, zsel, c):
        ref = (o - 1, zsel * SPLIT + c)
        return remote(part.at[ref], peers.at[ref], rs_s.at[ref], rs_r.at[ref], along_y(o))

    def cross(c):
        return remote(zsum.at[c], zpeer.at[c], rz_s.at[c], rz_r.at[c], across)

    for zsel in range(2):
        target = (zhi if zsel == 1 else 1 - zhi) * NY
        for c in range(SPLIT):
            for o in (2, 1, 3):
                part[o - 1, zsel * SPLIT + c] = share(target + (y + o) % NY, c).astype(BF16)
                exchange(o, zsel, c).start()
            acc[zsel, :, c * cut : (c + 1) * cut] = share(target + y, c).astype(BF16).astype(F32)
    for zsel in range(2):
        for c in range(SPLIT):
            total = acc[zsel, :, c * cut : (c + 1) * cut]
            for o in (1, 3, 2):
                exchange(o, zsel, c).wait_recv()
            for o in (1, 2, 3):
                total = total + peers[o - 1, zsel * SPLIT + c].astype(F32)
            if zsel == 0:
                zsum[c] = total.astype(BF16)
                cross(c).start()
            else:
                acc[1, :, c * cut : (c + 1) * cut] = total

    def sent(j, carry):
        for piece in range(2):
            @pl.when(has_up & (j <= p))
            def _():
                z_copy(piece, 0, j).wait_send()

            @pl.when(has_down & (j >= p))
            def _():
                z_copy(piece, 1, j).wait_send()

        return carry

    lax.fori_loop(0, NZ, sent, 0)
    for piece in range(2):
        eight, all_own = rows_of(piece, 0, NZ * depth), rows_of(piece, 0, NX * NZ * depth)
        for k in (1, 2, 3):
            remote(eight, eight, x_s.at[piece, k - 1], x_r.at[piece, k - 1, 0], along_x(k)).wait_send()
        remote(all_own, all_own, d_s.at[piece], own_r.at[piece], sibling).wait_send()
    tok_z.wait_send()
    for half in range(2):
        for o in (1, 2, 3):
            tok_y(half, o).wait_send()
    for zsel in range(2):
        for c in range(SPLIT):
            for o in (1, 2, 3):
                exchange(o, zsel, c).wait_send()

    @pl.when(seq < n_seq - 1)
    def _():
        hand_on.wait_send()

    for c in range(SPLIT):
        cross(c).wait()
        out[:, c * cut : (c + 1) * cut] = (acc[1, :, c * cut : (c + 1) * cut] + zpeer[c].astype(F32)).astype(BF16)


def local(tokens, norm_gain, w_qkv, conv_filter, w_out):
    rows, width = tokens.shape
    features = norm_gain.shape[0]
    depth = w_qkv.shape[1]
    groups = conv_filter.shape[0]
    dma = pltpu.SemaphoreType.DMA
    column = 2 * NZ * depth
    cut = width // SPLIT
    scratch = [
        pltpu.VMEM((3, features, width), BF16),
        pltpu.VMEM((2 * NY, rows, width), BF16),
        pltpu.VMEM((NX, rows, column), BF16),
        pltpu.VMEM((3, rows, width), F32),
        pltpu.VMEM((rows, width), BF16),
        pltpu.VMEM((rows, width), BF16),
        pltpu.VMEM((1, features), F32),
        pltpu.VMEM((groups, TAPS), F32),
        pltpu.VMEM((groups, TAPS), F32),
        pltpu.VMEM((groups, TAPS, TAPS), BF16),
        pltpu.VMEM((groups, TAPS, TAPS), BF16),
        pltpu.VMEM(w_out.shape, BF16),
        pltpu.VMEM((NY - 1, 2 * SPLIT, rows, cut), BF16),
        pltpu.VMEM((NY - 1, 2 * SPLIT, rows, cut), BF16),
        pltpu.VMEM((SPLIT, rows, cut), BF16),
        pltpu.VMEM((SPLIT, rows, cut), BF16),
    ]
    sems = [(5,), (2, 2, NZ), (2, NZ), (2, NX - 1), (2, NX - 1, NZ), (2,), (2, NX - 1, NZ), (2,)]
    sems += [(1,), (1,), (2, NY - 1), (2, NY - 1), (1,), (1,)]
    sems += [(NY - 1, 2 * SPLIT), (NY - 1, 2 * SPLIT), (SPLIT,), (SPLIT,)]
    hbm, vmem = pl.BlockSpec(memory_space=pl.ANY), pl.BlockSpec(memory_space=pltpu.VMEM)
    return pl.pallas_call(
        kernel,
        out_shape=jax.ShapeDtypeStruct((rows, width), BF16),
        in_specs=[hbm] * 5,
        out_specs=vmem,
        scratch_shapes=scratch + [dma(s) for s in sems],
        compiler_params=pltpu.CompilerParams(
            collective_id=0, has_side_effects=True, vmem_limit_bytes=60 * 1024 * 1024
        ),
        cost_estimate=pl.CostEstimate(flops=2300000000, bytes_accessed=20000000, transcendentals=0),
    )(tokens, norm_gain.reshape(1, features), w_qkv, conv_filter, w_out)


def solution(mesh):
    placed = (P("seq", "mp"), P(), P(None, "seq", "mp"), P("mp", None), P("mp", None))
    return jax.shard_map(
        local, mesh=mesh, in_specs=placed, out_specs=P("seq", "mp"), check_vma=False
    )
```

time: 123 us -> 122 us (level)
  local copies, waits for them, and re-layouts: 3.92 us -> 1.57 us
    unnamed x9 -> x1, local copies, waits for them, and re-layouts: 3.92 us -> 1.57 us
where the time goes in v2:
time: 122 us; the launch traced here: 121 us
  Pallas kernels  119 us (98%)
  local copies, waits for them, and re-layouts  1.57 us (1%)
    pallas_call x1, Pallas kernels, local(): pl.pallas_call(kernel, out_shape=jax.ShapeDtypeStruct((rows, width), BF16...  119 us

profile of v2, /device:TPU:1, one launch (start us, length us, event | category | flops | bytes accessed | tf_op | source)
XLA Modules:
  0.0 120.9 jit_solution(17525503012065661628)
XLA Ops:
  0.0 119.3 %shard_map.55 = bf16[128,512]{1,0:T(8,128)(2,1)} custom-call(bf16[128,512]{1,0:T(8,128)(2,1)} %tok_in.1, f32[1,4096]{1,0:T(1,128)} %bitcast.1, bf16[3,64,512]{2,1,0:T(8,128)(2,1)} %w_in.1, f32[32,128]{1,0:T(8,128)} %filt_in.1, bf16[512,4096]{1,0:T(8,128)(2,1)} %wout_in.1), custom_call_target="tpu_custom_call" | custom-call | flops 2300000000 | bytes 20000000 | tf_op jit(solution)/shard_map/pallas_call | solution.py:369
  119.4 1.6 %copy.7 = bf16[128,512]{1,0:T(8,128)(2,1)} copy(bf16[128,512]{1,0:T(8,128)(2,1)} %shard_map.55) | data formatting | bytes 262144

commit v3 on v2

v3 whole, which is shorter than its diff:
```python
import jax
import jax.numpy as jnp
from jax import lax
from jax.experimental import pallas as pl
from jax.experimental.pallas import tpu as pltpu
from jax.sharding import PartitionSpec as P

NX, NZ, NY = 4, 8, 4
TAPS = 128
TOKENS_AT = 3
SPLIT = 2
F32, BF16 = jnp.float32, jnp.bfloat16


def dot(a, b):
    return jnp.dot(a, b, preferred_element_type=F32)


def kernel(
    tok_in, gain_in, w_in, filt_in, wout_in, out,
    wbuf, tok, gath, scaled, acc, sends, arrivals, kvb, halo, gated, gain, filt, frev, tcur, tprev, wout,
    part, peers, zsum, zpeer,
    loc, z_s, z_r, d_s, d_r, tx_s, tx_r, q_s, q_r, tz_s, tz_r, ty_s, ty_r, hl_s, hl_r, rs_s, rs_r, rz_s, rz_r,
):
    seq, mp = lax.axis_index("seq"), lax.axis_index("mp")
    core, p, x = seq % 2, (seq // 2) % NZ, seq // (2 * NZ)
    zhi, y = mp // NY, mp % NY
    rows = tok_in.shape[0]
    depth = w_in.shape[1]
    width = w_in.shape[2]
    chunk = 2 * depth
    column = NZ * chunk
    cut = width // SPLIT
    sibling = (seq + 1 - 2 * core, mp)
    across = (seq, (mp + NY) % (2 * NY))
    n_seq = 2 * NZ * NX

    def along_x(k):
        return ((seq + 2 * NZ * k) % n_seq, mp)

    def along_z(d):
        return (seq + (2 if d == 0 else -2), mp)

    def along_y(o):
        return (seq, zhi * NY + (y + o) % NY)

    def remote(src, dst, s, r, dev):
        return pltpu.make_async_remote_copy(
            src_ref=src, dst_ref=dst, send_sem=s, recv_sem=r,
            device_id=dev, device_id_type=pl.DeviceIdType.MESH,
        )

    own_w = pl.ds(pl.multiple_of((2 * p + core) * depth, depth), depth)
    loads = [
        pltpu.make_async_copy(filt_in, filt, loc.at[0]),
        pltpu.make_async_copy(tok_in, tok.at[mp], loc.at[1]),
        pltpu.make_async_copy(w_in, wbuf.at[:, own_w, :], loc.at[2]),
        pltpu.make_async_copy(gain_in, gain, loc.at[3]),
        pltpu.make_async_copy(wout_in, wout, loc.at[4]),
    ]
    for load in loads:
        load.start()

    barrier = pltpu.get_barrier_semaphore()

    def greet(dev):
        pl.semaphore_signal(barrier, inc=1, device_id=dev, device_id_type=pl.DeviceIdType.MESH)

    for dev in [sibling, across] + [along_x(k) for k in (1, 2, 3)] + [along_y(o) for o in (1, 2, 3)]:
        greet(dev)
    has_up, has_down = p < NZ - 1, p > 0
    has_far = jnp.where(core == 0, seq > 0, seq < n_seq - 1)
    far = jnp.where(core == 0, seq - 1, seq + 1)

    @pl.when(has_up)
    def _():
        greet(along_z(0))

    @pl.when(has_down)
    def _():
        greet(along_z(1))

    @pl.when(has_far)
    def _():
        greet((far, mp))

    lane = lax.broadcasted_iota(jnp.int32, (TAPS, TAPS), 1)
    row = lax.broadcasted_iota(jnp.int32, (TAPS, TAPS), 0)
    flip = jnp.where(lane + row == TAPS - 1, 1.0, 0.0).astype(BF16)
    loads[0].wait()
    frev[...] = dot(filt[...].astype(BF16), flip)

    def build(g, carry):
        spread = jnp.broadcast_to(frev[pl.ds(g, 1), :], (TAPS, TAPS))
        turned = pltpu.roll(spread, 1, 1, stride=1, stride_axis=0)
        tcur[g] = jnp.where(lane <= row, turned, 0.0).astype(BF16)
        tprev[g] = jnp.where(lane > row, turned, 0.0).astype(BF16)
        return carry

    lax.fori_loop(0, filt.shape[0], build, 0)
    for load in loads[1:4]:
        load.wait()
    pl.semaphore_wait(
        barrier, 8 + has_up.astype(jnp.int32) + has_down.astype(jnp.int32) + has_far.astype(jnp.int32)
    )

    tok_z = remote(tok.at[mp], tok.at[mp], tz_s.at[0], tz_r.at[0], across)
    tok_z.start()

    def tok_y(half, o):
        m = mp if half == 0 else (mp + NY) % (2 * NY)
        return remote(tok.at[m], tok.at[m], ty_s.at[half, o - 1], ty_r.at[half, o - 1], along_y(o))

    def tok_y_arrival(half, o):
        m = (zhi if half == 0 else 1 - zhi) * NY + (y + NY - o) % NY
        return remote(tok.at[m], tok.at[m], ty_s.at[half, o - 1], ty_r.at[half, o - 1], along_y(o))

    for o in (2, 1, 3):
        tok_y(0, o).start()

    def tok_x(k):
        to = (x + k) % NX
        return remote(tok.at[pl.ds(2 * to, 2)], gath.at[k - 1], tx_s.at[k - 1], tx_r.at[k - 1], along_x(k))

    def tok_x_start(half):
        for k in (2, 1, 3):
            here = ((x + k) % NX) // 2 == zhi

            @pl.when(here if half == 0 else jnp.logical_not(here))
            def _():
                tok_x(k).start()

    def rows_of(piece, start, count):
        which = pl.ds(1, 2) if piece == 0 else pl.ds(0, 1)
        return wbuf.at[which, pl.ds(pl.multiple_of(start, depth), count), :]

    def block(piece, j, c):
        return rows_of(piece, (j * 2 + c) * depth, depth)

    def z_copy(piece, d, j):
        ref = block(piece, j, core)
        return remote(ref, ref, z_s.at[piece, d, j], z_r.at[piece, j], along_z(d))

    def d_copy(piece, j, c):
        ref = block(piece, j, c)
        return remote(ref, ref, d_s.at[piece], d_r.at[piece, j], sibling)

    fewer = jnp.minimum(p, NZ - 1 - p)

    def nth(n):
        paired = jnp.where(n % 2 == 1, p - (n + 1) // 2, p + (n + 1) // 2)
        rest = jnp.where(2 * p < NZ, p + n - fewer, p - n + fewer)
        return jnp.where(n <= 2 * fewer, paired, rest)

    def pass_on(piece, j, first):
        if not first:
            z_copy(piece, 0, j).wait_recv()

        @pl.when(has_up & (j <= p))
        def _():
            z_copy(piece, 0, j).start()

        @pl.when(has_down & (j >= p))
        def _():
            z_copy(piece, 1, j).start()

        d_copy(piece, j, core).start()

    def stage_z(piece, k):
        @pl.when(k == 0)
        def _():
            pass_on(piece, p, True)

        @pl.when((k > 0) & (p - k >= 0))
        def _():
            pass_on(piece, p - k, False)

        @pl.when((k > 0) & (p + k < NZ))
        def _():
            pass_on(piece, p + k, False)

    def loop(first, last, step):
        def one(n, carry):
            step(n)
            return carry

        lax.fori_loop(first, last, one, 0)

    kinds = ((1, 2), (0,))

    def pair(piece, n):
        at, lanes = [], []
        for j in (nth(2 * n), nth(2 * n + 1)):
            d_copy(piece, j, 1 - core).wait_recv()
            at.append(pl.ds(pl.multiple_of(j * chunk, chunk), chunk))
        return at

    def multiply(piece, n):
        at = pair(piece, n)
        lhs = jnp.concatenate([scaled[:, :, a].reshape(NX * rows, chunk) for a in at], axis=1)
        for i in kinds[piece]:
            product = dot(lhs, jnp.concatenate([wbuf[i, a, :] for a in at], axis=0))
            acc[i] += product.reshape(NX, rows, width)

    def send_sum(piece, k):
        which = pl.ds(1, 2) if piece == 0 else pl.ds(0, 1)
        return remote(
            sends.at[k - 1, which], arrivals.at[k - 1, which], q_s.at[piece, k - 1], q_r.at[piece, k - 1], along_x(k)
        )

    def multiply_last(piece, n):
        at = pair(piece, n)
        for k in (2, 1, 3, 0):
            lhs = jnp.concatenate([scaled[k, :, a] for a in at], axis=1)
            for i in kinds[piece]:
                total = acc[i, k] + dot(lhs, jnp.concatenate([wbuf[i, a, :] for a in at], axis=0))
                if k > 0:
                    sends[k - 1, i] = total.astype(BF16)
                else:
                    acc[i, 0] = total
            if k > 0:
                send_sum(piece, k).start()

    def collect_sum(i):
        total = acc[i, 0]
        for k in (1, 2, 3):
            total = total + arrivals[k - 1, i].astype(F32)
        return (total * factor).astype(BF16).astype(F32)

    loop(0, 2, lambda k: stage_z(0, k))
    acc[...] = jnp.zeros_like(acc)
    for o in (1, 3, 2):
        tok_y_arrival(0, o).wait_recv()
    tok_x_start(0)
    loop(2, TOKENS_AT, lambda k: stage_z(0, k))
    tok_z.wait_recv()
    for o in (2, 1, 3):
        tok_y(1, o).start()
    loop(TOKENS_AT, TOKENS_AT + 2, lambda k: stage_z(0, k))
    for o in (1, 3, 2):
        tok_y_arrival(1, o).wait_recv()
    tok_x_start(1)
    loop(TOKENS_AT + 2, NZ, lambda k: stage_z(0, k))
    stage_z(1, 0)

    squares = jnp.zeros((rows, 128), F32)
    for m in range(2 * NY):
        for c in range(width // 128):
            v = tok[m, :, c * 128 : (c + 1) * 128].astype(F32)
            squares = squares + v * v
    factor = lax.rsqrt(jnp.sum(squares, axis=1, keepdims=True) / (2 * NY * width) + 1e-05)
    for h in range(2):
        g = gain[:, pl.ds(pl.multiple_of((2 * x + h) * width, width), width)]
        at = slice(h * width, (h + 1) * width)
        scaled[0, :, at] = (tok[2 * x + h].astype(F32) * g).astype(BF16)
    for k in (1, 3, 2):
        tok_x(k).wait_recv()
        for h in range(2):
            g = gain[:, pl.ds(pl.multiple_of((2 * x + h) * width, width), width)]
            at = slice(h * width, (h + 1) * width)
            scaled[NX - k, :, at] = (gath[k - 1, h].astype(F32) * g).astype(BF16)

    def middle(n):
        multiply(0, n)
        stage_z(1, n + 1)

    loop(0, NZ // 2 - 1, middle)
    multiply_last(0, NZ // 2 - 1)
    loop(NZ // 2, NZ, lambda k: stage_z(1, k))
    loop(0, NZ // 2 - 1, lambda n: multiply(1, n))
    multiply_last(1, NZ // 2 - 1)

    for k in (1, 3, 2):
        send_sum(0, k).wait_recv()
    kvb[...] = (collect_sum(1) * collect_sum(2)).astype(BF16)
    hand_on = remote(kvb, halo, hl_s.at[0], hl_r.at[0], ((seq + 1) % n_seq, mp))

    @pl.when(seq < n_seq - 1)
    def _():
        hand_on.start()

    @pl.when(seq == 0)
    def _():
        halo[...] = jnp.zeros_like(halo)

    groups = filt.shape[0]
    of_lane = lane // (width // groups)
    per_tile = 128 // (width // groups)

    def convolve(mats, source, t):
        lhs = mats[t * per_tile : (t + 1) * per_tile].reshape(per_tile * TAPS, TAPS)
        wide = dot(lhs, source[:, t * 128 : (t + 1) * 128])
        total = jnp.zeros((TAPS, 128), F32)
        for g in range(per_tile):
            total = jnp.where(of_lane == g, wide[g * TAPS : (g + 1) * TAPS], total)
        return total

    for t in range(width // 128):
        acc[1, 0, :, t * 128 : (t + 1) * 128] = convolve(tcur, kvb, t)

    @pl.when(seq > 0)
    def _():
        hand_on.wait_recv()

    for t in range(width // 128):
        acc[1, 0, :, t * 128 : (t + 1) * 128] += convolve(tprev, halo, t)
    loads[4].wait()
    for k in (1, 3, 2):
        send_sum(1, k).wait_recv()
    gated[...] = (collect_sum(0) * acc[1, 0]).astype(BF16)

    def share(m, c):
        return dot(gated[...], wout[:, pl.ds(pl.multiple_of(m * width + c * cut, cut), cut)])

    def exchange(o, zsel, c):
        ref = (o - 1, zsel * SPLIT + c)
        return remote(part.at[ref], peers.at[ref], rs_s.at[ref], rs_r.at[ref], along_y(o))

    def cross(c):
        return remote(zsum.at[c], zpeer.at[c], rz_s.at[c], rz_r.at[c], across)

    def hand_out(zsel, c):
        target = (zhi if zsel == 1 else 1 - zhi) * NY
        for o in (2, 1, 3):
            part[o - 1, zsel * SPLIT + c] = share(target + (y + o) % NY, c).astype(BF16)
            exchange(o, zsel, c).start()

    def keep(zsel, c):
        own = share((zhi if zsel == 1 else 1 - zhi) * NY + y, c)
        acc[1, 1 + zsel, :, c * cut : (c + 1) * cut] = own.astype(BF16).astype(F32)

    def collect(zsel, c):
        total = acc[1, 1 + zsel, :, c * cut : (c + 1) * cut]
        for o in (1, 3, 2):
            exchange(o, zsel, c).wait_recv()
        for o in (1, 2, 3):
            total = total + peers[o - 1, zsel * SPLIT + c].astype(F32)
        return total

    for c in range(SPLIT):
        hand_out(0, c)
    for c in range(SPLIT):
        keep(0, c)
    for c in range(SPLIT):
        zsum[c] = collect(0, c).astype(BF16)
        cross(c).start()
    for c in range(SPLIT):
        hand_out(1, c)
        keep(1, c)
    for c in range(SPLIT):
        acc[1, 2, :, c * cut : (c + 1) * cut] = collect(1, c)

    def sent(j, carry):
        for piece in range(2):
            @pl.when(has_up & (j <= p))
            def _():
                z_copy(piece, 0, j).wait_send()

            @pl.when(has_down & (j >= p))
            def _():
                z_copy(piece, 1, j).wait_send()

        return carry

    lax.fori_loop(0, NZ, sent, 0)
    for piece in range(2):
        eight = rows_of(piece, 0, NZ * depth)
        remote(eight, eight, d_s.at[piece], d_r.at[piece, 0], sibling).wait_send()
        for k in (1, 2, 3):
            send_sum(piece, k).wait_send()
    for k in (1, 2, 3):
        tok_x(k).wait_send()
    tok_z.wait_send()
    for half in range(2):
        for o in (1, 2, 3):
            tok_y(half, o).wait_send()
    for zsel in range(2):
        for c in range(SPLIT):
            for o in (1, 2, 3):
                exchange(o, zsel, c).wait_send()

    @pl.when(seq < n_seq - 1)
    def _():
        hand_on.wait_send()

    for c in range(SPLIT):
        cross(c).wait()
        out[:, c * cut : (c + 1) * cut] = (acc[1, 2, :, c * cut : (c + 1) * cut] + zpeer[c].astype(F32)).astype(BF16)


def local(tokens, norm_gain, w_qkv, conv_filter, w_out):
    rows, width = tokens.shape
    features = norm_gain.shape[0]
    depth = w_qkv.shape[1]
    groups = conv_filter.shape[0]
    dma = pltpu.SemaphoreType.DMA
    column = 2 * NZ * depth
    cut = width // SPLIT
    scratch = [
        pltpu.VMEM((3, column, width), BF16),
        pltpu.VMEM((2 * NY, rows, width), BF16),
        pltpu.VMEM((NX - 1, 2, rows, width), BF16),
        pltpu.VMEM((NX, rows, column), BF16),
        pltpu.VMEM((3, NX, rows, width), F32),
        pltpu.VMEM((NX - 1, 3, rows, width), BF16),
        pltpu.VMEM((NX - 1, 3, rows, width), BF16),
        pltpu.VMEM((rows, width), BF16),
        pltpu.VMEM((rows, width), BF16),
        pltpu.VMEM((rows, width), BF16),
        pltpu.VMEM((1, features), F32),
        pltpu.VMEM((groups, TAPS), F32),
        pltpu.VMEM((groups, TAPS), F32),
        pltpu.VMEM((groups, TAPS, TAPS), BF16),
        pltpu.VMEM((groups, TAPS, TAPS), BF16),
        pltpu.VMEM(w_out.shape, BF16),
        pltpu.VMEM((NY - 1, 2 * SPLIT, rows, cut), BF16),
        pltpu.VMEM((NY - 1, 2 * SPLIT, rows, cut), BF16),
        pltpu.VMEM((SPLIT, rows, cut), BF16),
        pltpu.VMEM((SPLIT, rows, cut), BF16),
    ]
    sems = [(5,), (2, 2, NZ), (2, NZ), (2,), (2, NZ), (NX - 1,), (NX - 1,), (2, NX - 1), (2, NX - 1)]
    sems += [(1,), (1,), (2, NY - 1), (2, NY - 1), (1,), (1,)]
    sems += [(NY - 1, 2 * SPLIT), (NY - 1, 2 * SPLIT), (SPLIT,), (SPLIT,)]
    hbm, vmem = pl.BlockSpec(memory_space=pl.ANY), pl.BlockSpec(memory_space=pltpu.VMEM)
    return pl.pallas_call(
        kernel,
        out_shape=jax.ShapeDtypeStruct((rows, width), BF16),
        in_specs=[hbm] * 5,
        out_specs=vmem,
        scratch_shapes=scratch + [dma(s) for s in sems],
        compiler_params=pltpu.CompilerParams(
            collective_id=0, has_side_effects=True, vmem_limit_bytes=60 * 1024 * 1024
        ),
        cost_estimate=pl.CostEstimate(flops=2300000000, bytes_accessed=20000000, transcendentals=0),
    )(tokens, norm_gain.reshape(1, features), w_qkv, conv_filter, w_out)


def solution(mesh):
    placed = (P("seq", "mp"), P(), P(None, "seq", "mp"), P("mp", None), P("mp", None))
    return jax.shard_map(
        local, mesh=mesh, in_specs=placed, out_specs=P("seq", "mp"), check_vma=False
    )
```

time: 122 us -> 114 us (0.934)
  Pallas kernels: 119 us -> 112 us
    pallas_call x1, Pallas kernels: 119 us -> 112 us  [local(): pl.pallas_call(kernel, out_shape=jax.ShapeDtypeStruct((rows, width), BF16...]
where the time goes in v3:
time: 114 us
  Pallas kernels  112 us (98%)
  local copies, waits for them, and re-layouts  1.57 us (1%)
    pallas_call x1, Pallas kernels, local(): pl.pallas_call(kernel, out_shape=jax.ShapeDtypeStruct((rows, width), BF16...  112 us

profile of v3, /device:TPU:1, one launch (start us, length us, event | category | flops | bytes accessed | tf_op | source)
XLA Modules:
  0.0 114.0 jit_solution(16488081222906451538)
XLA Ops:
  0.0 112.4 %shard_map.55 = bf16[128,512]{1,0:T(8,128)(2,1)} custom-call(bf16[128,512]{1,0:T(8,128)(2,1)} %tok_in.1, f32[1,4096]{1,0:T(1,128)} %bitcast.1, bf16[3,64,512]{2,1,0:T(8,128)(2,1)} %w_in.1, f32[32,128]{1,0:T(8,128)} %filt_in.1, bf16[512,4096]{1,0:T(8,128)(2,1)} %wout_in.1), custom_call_target="tpu_custom_call" | custom-call | flops 2300000000 | bytes 20000000 | tf_op jit(solution)/shard_map/pallas_call | solution.py:425
  112.5 1.6 %copy.7 = bf16[128,512]{1,0:T(8,128)(2,1)} copy(bf16[128,512]{1,0:T(8,128)(2,1)} %shard_map.55) | data formatting | bytes 262144

commit v4 on v3

--- a/solution.py
+++ b/solution.py
@@ -7,6 +7,7 @@
 
 NX, NZ, NY = 4, 8, 4
 TAPS = 128
+LAG = 2
 TOKENS_AT = 3
 SPLIT = 2
 F32, BF16 = jnp.float32, jnp.bfloat16
@@ -130,20 +131,16 @@
             def _():
                 tok_x(k).start()
 
-    def rows_of(piece, start, count):
-        which = pl.ds(1, 2) if piece == 0 else pl.ds(0, 1)
-        return wbuf.at[which, pl.ds(pl.multiple_of(start, depth), count), :]
-
-    def block(piece, j, c):
-        return rows_of(piece, (j * 2 + c) * depth, depth)
-
-    def z_copy(piece, d, j):
-        ref = block(piece, j, core)
-        return remote(ref, ref, z_s.at[piece, d, j], z_r.at[piece, j], along_z(d))
-
-    def d_copy(piece, j, c):
-        ref = block(piece, j, c)
-        return remote(ref, ref, d_s.at[piece], d_r.at[piece, j], sibling)
+    def block(i, j, c):
+        return wbuf.at[i, pl.ds(pl.multiple_of((j * 2 + c) * depth, depth), depth), :]
+
+    def z_copy(i, d, j):
+        ref = block(i, j, core)
+        return remote(ref, ref, z_s.at[i, d, j], z_r.at[i, j], along_z(d))
+
+    def d_copy(i, j, c):
+        ref = block(i, j, c)
+        return remote(ref, ref, d_s.at[i], d_r.at[i, j], sibling)
 
     fewer = jnp.minimum(p, NZ - 1 - p)
 
@@ -152,32 +149,40 @@
         rest = jnp.where(2 * p < NZ, p + n - fewer, p - n + fewer)
         return jnp.where(n <= 2 * fewer, paired, rest)
 
-    def pass_on(piece, j, first):
+    def pass_on(i, j, first):
         if not first:
-            z_copy(piece, 0, j).wait_recv()
+            z_copy(i, 0, j).wait_recv()
 
         @pl.when(has_up & (j <= p))
         def _():
-            z_copy(piece, 0, j).start()
+            z_copy(i, 0, j).start()
 
         @pl.when(has_down & (j >= p))
         def _():
-            z_copy(piece, 1, j).start()
-
-        d_copy(piece, j, core).start()
-
-    def stage_z(piece, k):
+            z_copy(i, 1, j).start()
+
+        d_copy(i, j, core).start()
+
+    def stage_z(i, k):
         @pl.when(k == 0)
         def _():
-            pass_on(piece, p, True)
+            pass_on(i, p, True)
 
         @pl.when((k > 0) & (p - k >= 0))
         def _():
-            pass_on(piece, p - k, False)
+            pass_on(i, p - k, False)
 
         @pl.when((k > 0) & (p + k < NZ))
         def _():
-            pass_on(piece, p + k, False)
+            pass_on(i, p + k, False)
+
+    def step_z(k):
+        stage_z(1, k)
+        stage_z(2, k)
+
+        @pl.when(k >= LAG)
+        def _():
+            stage_z(0, k - LAG)
 
     def loop(first, last, step):
         def one(n, carry):
@@ -191,7 +196,8 @@
     def pair(piece, n):
         at, lanes = [], []
         for j in (nth(2 * n), nth(2 * n + 1)):
-            d_copy(piece, j, 1 - core).wait_recv()
+            for i in kinds[piece]:
+                d_copy(i, j, 1 - core).wait_recv()
             at.append(pl.ds(pl.multiple_of(j * chunk, chunk), chunk))
         return at
 
@@ -227,21 +233,20 @@
             total = total + arrivals[k - 1, i].astype(F32)
         return (total * factor).astype(BF16).astype(F32)
 
-    loop(0, 2, lambda k: stage_z(0, k))
+    loop(0, 2, step_z)
     acc[...] = jnp.zeros_like(acc)
     for o in (1, 3, 2):
         tok_y_arrival(0, o).wait_recv()
     tok_x_start(0)
-    loop(2, TOKENS_AT, lambda k: stage_z(0, k))
+    loop(2, TOKENS_AT, step_z)
     tok_z.wait_recv()
     for o in (2, 1, 3):
         tok_y(1, o).start()
-    loop(TOKENS_AT, TOKENS_AT + 2, lambda k: stage_z(0, k))
+    loop(TOKENS_AT, TOKENS_AT + 2, step_z)
     for o in (1, 3, 2):
         tok_y_arrival(1, o).wait_recv()
     tok_x_start(1)
-    loop(TOKENS_AT + 2, NZ, lambda k: stage_z(0, k))
-    stage_z(1, 0)
+    loop(TOKENS_AT + 2, NZ, step_z)
 
     squares = jnp.zeros((rows, 128), F32)
     for m in range(2 * NY):
@@ -262,11 +267,12 @@
 
     def middle(n):
         multiply(0, n)
-        stage_z(1, n + 1)
-
-    loop(0, NZ // 2 - 1, middle)
+        stage_z(0, NZ - LAG + n)
+
+    loop(0, min(LAG, NZ // 2 - 1), middle)
+    loop(min(LAG, NZ // 2 - 1), NZ // 2 - 1, lambda n: multiply(0, n))
     multiply_last(0, NZ // 2 - 1)
-    loop(NZ // 2, NZ, lambda k: stage_z(1, k))
+    loop(NZ - LAG + min(LAG, NZ // 2 - 1), NZ, lambda k: stage_z(0, k))
     loop(0, NZ // 2 - 1, lambda n: multiply(1, n))
     multiply_last(1, NZ // 2 - 1)
 
@@ -351,21 +357,22 @@
         acc[1, 2, :, c * cut : (c + 1) * cut] = collect(1, c)
 
     def sent(j, carry):
-        for piece in range(2):
+        for i in range(3):
             @pl.when(has_up & (j <= p))
             def _():
-                z_copy(piece, 0, j).wait_send()
+                z_copy(i, 0, j).wait_send()
 
             @pl.when(has_down & (j >= p))
             def _():
-                z_copy(piece, 1, j).wait_send()
+                z_copy(i, 1, j).wait_send()
 
         return carry
 
     lax.fori_loop(0, NZ, sent, 0)
+    for i in range(3):
+        eight = wbuf.at[i, pl.ds(0, NZ * depth), :]
+        remote(eight, eight, d_s.at[i], d_r.at[i, 0], sibling).wait_send()
     for piece in range(2):
-        eight = rows_of(piece, 0, NZ * depth)
-        remote(eight, eight, d_s.at[piece], d_r.at[piece, 0], sibling).wait_send()
         for k in (1, 2, 3):
             send_sum(piece, k).wait_send()
     for k in (1, 2, 3):
@@ -418,7 +425,7 @@
         pltpu.VMEM((SPLIT, rows, cut), BF16),
         pltpu.VMEM((SPLIT, rows, cut), BF16),
     ]
-    sems = [(5,), (2, 2, NZ), (2, NZ), (2,), (2, NZ), (NX - 1,), (NX - 1,), (2, NX - 1), (2, NX - 1)]
+    sems = [(5,), (3, 2, NZ), (3, NZ), (3,), (3, NZ), (NX - 1,), (NX - 1,), (2, NX - 1), (2, NX - 1)]
     sems += [(1,), (1,), (2, NY - 1), (2, NY - 1), (1,), (1,)]
     sems += [(NY - 1, 2 * SPLIT), (NY - 1, 2 * SPLIT), (SPLIT,), (SPLIT,)]
     hbm, vmem = pl.BlockSpec(memory_space=pl.ANY), pl.BlockSpec(memory_space=pltpu.VMEM)

time: 114 us -> 103 us (0.904)
  the two profiles are of different devices: /device:TPU:1 before, /device:TPU:130 now
where the time goes in v4:
time: 103 us
  Pallas kernels  101 us (98%)
  local copies, waits for them, and re-layouts  1.57 us (2%)
    pallas_call x1, Pallas kernels, local(): pl.pallas_call(kernel, out_shape=jax.ShapeDtypeStruct((rows, width), BF16...  101 us

profile of v4, /device:TPU:130, one launch (start us, length us, event | category | flops | bytes accessed | tf_op | source)
XLA Modules:
  0.0 102.7 jit_solution(942136297052846733)
XLA Ops:
  0.0 101.2 %shard_map.55 = bf16[128,512]{1,0:T(8,128)(2,1)} custom-call(bf16[128,512]{1,0:T(8,128)(2,1)} %tok_in.1, f32[1,4096]{1,0:T(1,128)} %bitcast.1, bf16[3,64,512]{2,1,0:T(8,128)(2,1)} %w_in.1, f32[32,128]{1,0:T(8,128)} %filt_in.1, bf16[512,4096]{1,0:T(8,128)(2,1)} %wout_in.1), custom_call_target="tpu_custom_call" | custom-call | flops 2300000000 | bytes 20000000 | tf_op jit(solution)/shard_map/pallas_call | solution.py:432
  101.2 1.6 %copy.7 = bf16[128,512]{1,0:T(8,128)(2,1)} copy(bf16[128,512]{1,0:T(8,128)(2,1)} %shard_map.55) | data formatting | bytes 262144

commit v5 on v4

--- a/solution.py
+++ b/solution.py
@@ -8,7 +8,7 @@
 NX, NZ, NY = 4, 8, 4
 TAPS = 128
 LAG = 2
-TOKENS_AT = 3
+TOKENS_AT = 2
 SPLIT = 2
 F32, BF16 = jnp.float32, jnp.bfloat16
 
@@ -242,11 +242,11 @@
     tok_z.wait_recv()
     for o in (2, 1, 3):
         tok_y(1, o).start()
-    loop(TOKENS_AT, TOKENS_AT + 2, step_z)
+    loop(TOKENS_AT, TOKENS_AT + 1, step_z)
     for o in (1, 3, 2):
         tok_y_arrival(1, o).wait_recv()
     tok_x_start(1)
-    loop(TOKENS_AT + 2, NZ, step_z)
+    loop(TOKENS_AT + 1, NZ, step_z)
 
     squares = jnp.zeros((rows, 128), F32)
     for m in range(2 * NY):

time: 103 us -> 102 us (level)
  the two profiles are of different devices: /device:TPU:130 before, /device:TPU:1 now
where the time goes in v5:
time: 102 us; the launch traced here: 101 us
  Pallas kernels  99.7 us (98%)
  local copies, waits for them, and re-layouts  1.57 us (2%)
    pallas_call x1, Pallas kernels, local(): pl.pallas_call(kernel, out_shape=jax.ShapeDtypeStruct((rows, width), BF16...  99.7 us

profile of v5, /device:TPU:1, one launch (start us, length us, event | category | flops | bytes accessed | tf_op | source)
XLA Modules:
  0.0 101.3 jit_solution(13069674610942313786)
XLA Ops:
  0.0 99.7 %shard_map.55 = bf16[128,512]{1,0:T(8,128)(2,1)} custom-call(bf16[128,512]{1,0:T(8,128)(2,1)} %tok_in.1, f32[1,4096]{1,0:T(1,128)} %bitcast.1, bf16[3,64,512]{2,1,0:T(8,128)(2,1)} %w_in.1, f32[32,128]{1,0:T(8,128)} %filt_in.1, bf16[512,4096]{1,0:T(8,128)(2,1)} %wout_in.1), custom_call_target="tpu_custom_call" | custom-call | flops 2300000000 | bytes 20000000 | tf_op jit(solution)/shard_map/pallas_call | solution.py:432
  99.7 1.6 %copy.7 = bf16[128,512]{1,0:T(8,128)(2,1)} copy(bf16[128,512]{1,0:T(8,128)(2,1)} %shard_map.55) | data formatting | bytes 262144

commit v6 on v5

--- a/solution.py
+++ b/solution.py
@@ -8,7 +8,7 @@
 NX, NZ, NY = 4, 8, 4
 TAPS = 128
 LAG = 2
-TOKENS_AT = 2
+TOKENS_AT, TURN_AT, SCALE_AT = 2, 3, 7
 SPLIT = 2
 F32, BF16 = jnp.float32, jnp.bfloat16
 
@@ -233,20 +233,20 @@
             total = total + arrivals[k - 1, i].astype(F32)
         return (total * factor).astype(BF16).astype(F32)
 
-    loop(0, 2, step_z)
+    loop(0, 1, step_z)
     acc[...] = jnp.zeros_like(acc)
     for o in (1, 3, 2):
         tok_y_arrival(0, o).wait_recv()
     tok_x_start(0)
-    loop(2, TOKENS_AT, step_z)
+    loop(1, TOKENS_AT, step_z)
     tok_z.wait_recv()
     for o in (2, 1, 3):
         tok_y(1, o).start()
-    loop(TOKENS_AT, TOKENS_AT + 1, step_z)
+    loop(TOKENS_AT, TURN_AT, step_z)
     for o in (1, 3, 2):
         tok_y_arrival(1, o).wait_recv()
     tok_x_start(1)
-    loop(TOKENS_AT + 1, NZ, step_z)
+    loop(TURN_AT, SCALE_AT, step_z)
 
     squares = jnp.zeros((rows, 128), F32)
     for m in range(2 * NY):
@@ -265,15 +265,14 @@
             at = slice(h * width, (h + 1) * width)
             scaled[NX - k, :, at] = (gath[k - 1, h].astype(F32) * g).astype(BF16)
 
-    def middle(n):
-        multiply(0, n)
-        stage_z(0, NZ - LAG + n)
-
-    loop(0, min(LAG, NZ // 2 - 1), middle)
-    loop(min(LAG, NZ // 2 - 1), NZ // 2 - 1, lambda n: multiply(0, n))
+    loop(0, (SCALE_AT - 2) // 2, lambda n: multiply(0, n))
+    loop(SCALE_AT, NZ - 1, step_z)
+    loop((SCALE_AT - 2) // 2, NZ // 2 - 1, lambda n: multiply(0, n))
+    loop(NZ - 1, NZ, step_z)
     multiply_last(0, NZ // 2 - 1)
-    loop(NZ - LAG + min(LAG, NZ // 2 - 1), NZ, lambda k: stage_z(0, k))
+    loop(NZ - LAG, NZ - 1, lambda k: stage_z(0, k))
     loop(0, NZ // 2 - 1, lambda n: multiply(1, n))
+    stage_z(0, NZ - 1)
     multiply_last(1, NZ // 2 - 1)
 
     for k in (1, 3, 2):

time: 102 us -> 102 us (level)
  no operation moved by 1% of the time
where the time goes in v6:
time: 102 us
  Pallas kernels  100 us (98%)
  local copies, waits for them, and re-layouts  1.57 us (2%)
    pallas_call x1, Pallas kernels, local(): pl.pallas_call(kernel, out_shape=jax.ShapeDtypeStruct((rows, width), BF16...  100 us

profile of v6, /device:TPU:1, one launch (start us, length us, event | category | flops | bytes accessed | tf_op | source)
XLA Modules:
  0.0 102.0 jit_solution(8897940074913954247)
XLA Ops:
  0.0 100.4 %shard_map.55 = bf16[128,512]{1,0:T(8,128)(2,1)} custom-call(bf16[128,512]{1,0:T(8,128)(2,1)} %tok_in.1, f32[1,4096]{1,0:T(1,128)} %bitcast.1, bf16[3,64,512]{2,1,0:T(8,128)(2,1)} %w_in.1, f32[32,128]{1,0:T(8,128)} %filt_in.1, bf16[512,4096]{1,0:T(8,128)(2,1)} %wout_in.1), custom_call_target="tpu_custom_call" | custom-call | flops 2300000000 | bytes 20000000 | tf_op jit(solution)/shard_map/pallas_call | solution.py:431
  100.4 1.6 %copy.7 = bf16[128,512]{1,0:T(8,128)(2,1)} copy(bf16[128,512]{1,0:T(8,128)(2,1)} %shard_map.55) | data formatting | bytes 262144
